TPU v7x, 128 devices: a whole 4x4x4 slice. The times are simulated.
128 devices in a mesh: row: 8 (over x, y_lo), col: 16 (over y_hi, z, core).
Axes of the slice: x: 4, y: 4 (y_hi: 2, y_lo: 2; y = y_hi * 2 + y_lo), z: 4, core: 2. Of those that a mesh axis runs over, the one named last changes fastest.
Arguments:
- left_act: bfloat16 [512, 512, 32], P(None, ('row', 'col')), may hold values from -24 to 24
- right_act: bfloat16 [512, 512, 32], P('row', 'col'), may hold values from -24 to 24
- proj_weight: bfloat16 [1024, 128], replicated, may hold values from -0.1875 to 0.1875
- proj_bias: float32 [128], replicated, may hold values from -6 to 6
Outputs:
- pair_update: float32 [512, 512, 128], P('row', 'col')
All inputs are finite; a program needn't handle non-finite values.
Results may differ from a plain program's by a relative error of at most 0.0016.
Values may be sent and summed in bfloat16 or wider, within the bound.
A program may use at most 64 MiB of HBM per device.

v0:
```python
import jax
import jax.numpy as jnp
from jax import lax
from jax.sharding import PartitionSpec as P


def tile_rows(left_rows_all, right_whole, weight_three, proj_bias):
    seq_count = right_whole.shape[0]
    row_count = left_rows_all.shape[1]
    channels = left_rows_all.shape[2]
    col_count = right_whole.shape[1]
    pair_width = weight_three.shape[2]
    right_flat = right_whole.reshape(seq_count, col_count * channels)
    left_major = jnp.transpose(left_rows_all, (2, 0, 1))
    total = jnp.zeros((row_count * col_count, pair_width), jnp.float32)
    for channel in range(channels):
        outer_sum = lax.dot_general(
            left_major[channel],
            right_flat,
            (((0,), (0,)), ((), ())),
            preferred_element_type=jnp.float32,
        )
        outer_mean = (outer_sum / seq_count).astype(jnp.bfloat16)
        outer_flat = outer_mean.reshape(row_count * col_count, channels)
        total = total + jnp.dot(
            outer_flat, weight_three[channel], preferred_element_type=jnp.float32
        )
    return (total + proj_bias).reshape(row_count, col_count, pair_width)


def on_device(left_act, right_act, proj_weight, proj_bias):
    channels = left_act.shape[2]
    weight_three = proj_weight.reshape(channels, channels, proj_weight.shape[1])
    right_whole = lax.all_gather(right_act, "row", axis=0, tiled=True)
    left_whole = lax.all_gather(left_act, "col", axis=1, tiled=True)
    return tile_rows(left_whole, right_whole, weight_three, proj_bias)


def solution(mesh):
    return jax.shard_map(
        on_device,
        mesh=mesh,
        in_specs=(P(None, ("row", "col"), None), P("row", "col", None), P(), P()),
        out_specs=P("row", "col", None),
        check_vma=False,
    )
```

profile of v0, /device:TPU:1, one launch (start us, length us, event | category | flops | bytes accessed | tf_op | source)
XLA Modules:
  0.0 242.6 jit_solution(5219703723267538371)
XLA Ops:
  6.5 2.5 %copy.9 = bf16[64,32,32]{2,1,0:T(8,128)(2,1)} copy(bf16[64,32,32]{0,2,1:T(8,128)(2,1)} %param.5) | data formatting | bytes 262144 | tf_op args[1]
  9.1 0.7 all-gather.3.cloned.1.call-update
  9.8 92.3 %all-gather.5.cloned.1.call-done = bf16[512,32,32]{2,1,0:T(8,128)(2,1)} async-done(((bf16[64,32,32]{2,1,0:T(8,128)(2,1)}), bf16[512,32,32]{2,1,0:T(8,128)(2,1)}) %all-gather.5.cloned.1.call-update) | async-done | bytes 1048592 | tf_op jit(solution)/shard_map/all_gather | solution.py:34
  102.1 4.4 %copy.10 = bf16[512,32,32]{0,2,1:T(8,128)(2,1)S(1)} copy(bf16[512,32,32]{2,1,0:T(8,128)(2,1)} %all-gather.5.cloned.1.call-done) | data formatting | bytes 2097152 | tf_op jit(solution)/shard_map/all_gather | solution.py:34
  106.5 48.6 %all-gather.3.cloned.1.call-done = bf16[512,64,32]{0,2,1:T(8,128)(2,1)} async-done(((bf16[512,4,32]{0,2,1:T(8,128)(2,1)}), bf16[512,64,32]{0,2,1:T(8,128)(2,1)}) %all-gather.3.cloned.1.call-update) | async-done | bytes 2097168 | tf_op jit(solution)/shard_map/all_gather | solution.py:35
  155.2 2.8 %copy.12 = bf16[512,64,32]{0,1,2:T(8,128)(2,1)S(1)} copy(bf16[512,64,32]{0,2,1:T(8,128)(2,1)} %all-gather.3.cloned.1.call-done) | data formatting | bytes 4194304 | tf_op jit(solution)/shard_map/all_gather | solution.py:35
  157.9 1.1 fusion.1
  159.0 1.1 fusion.2
  160.1 1.1 fusion.3
  161.2 1.1 fusion.4
  162.3 1.1 fusion.5
  163.4 1.1 fusion.6
  164.5 1.1 fusion.7
  165.6 1.1 fusion.8
  166.7 1.1 fusion.9
  167.8 1.1 fusion.10
  168.9 1.1 fusion.11
  170.0 1.1 fusion.12
  178.2 1.1 fusion.29
  180.7 2.1 reshape.169
  182.8 2.1 reshape.170
  185.0 2.1 reshape.171
  187.1 2.1 reshape.172
  189.2 1.2 reshape.173
  190.4 1.2 reshape.174
  191.6 1.2 reshape.175
  192.8 1.2 reshape.176
  193.9 1.2 reshape.177
  195.1 1.2 reshape.178
  196.3 1.2 reshape.179
  197.4 1.1 reshape.180
  198.6 1.2 reshape.181
  199.8 1.2 reshape.182
  200.9 1.3 reshape.183
  202.3 1.2 reshape.184
  203.5 1.2 reshape.185
  204.7 1.2 reshape.186
  205.9 1.2 reshape.187
  207.0 1.2 reshape.188
  208.2 1.2 reshape.189
  209.4 1.1 reshape.190
  210.5 1.2 reshape.191
  211.7 1.2 reshape.192
  212.9 1.2 reshape.193
  216.3 1.2 reshape.200
  217.4 1.4 fusion.64
  218.8 1.4 convolution_add_fusion.30
  234.5 1.2 fusion
  (127 shorter events, 24.7 us)
Async XLA Ops:
  6.5 95.6 %all-gather.5.cloned.1.call-start = ((), (), s32[]{:S(2)}) async-start(), calls=%async_computation.1 | async-start | bytes 4718592 | tf_op jit(solution)/shard_map/all_gather | solution.py:34
  9.0 146.1 %all-gather.3.cloned.1.call-start = ((), (), s32[]{:S(2)}) async-start(), calls=%async_computation | async-start | bytes 2228224 | tf_op jit(solution)/shard_map/all_gather | solution.py:35
  180.7 8.6 %copy-start.32 = (bf16[64,1024]{1,0:T(8,128)(2,1)S(1)}, bf16[64,1024]{1,0:T(8,128)(2,1)}, u32[]{:S(2)}) copy-start(bf16[64,1024]{1,0:T(8,128)(2,1)} %fusion.5) | copy-start | bytes 393220
  180.7 9.8 %copy-start.31 = (bf16[64,1024]{1,0:T(8,128)(2,1)S(1)}, bf16[64,1024]{1,0:T(8,128)(2,1)}, u32[]{:S(2)}) copy-start(bf16[64,1024]{1,0:T(8,128)(2,1)} %fusion.6) | copy-start | bytes 393220
  180.7 10.9 %copy-start.30 = (bf16[64,1024]{1,0:T(8,128)(2,1)S(1)}, bf16[64,1024]{1,0:T(8,128)(2,1)}, u32[]{:S(2)}) copy-start(bf16[64,1024]{1,0:T(8,128)(2,1)} %fusion.7) | copy-start | bytes 393220
  182.8 9.9 %copy-start.29 = (bf16[64,1024]{1,0:T(8,128)(2,1)S(1)}, bf16[64,1024]{1,0:T(8,128)(2,1)}, u32[]{:S(2)}) copy-start(bf16[64,1024]{1,0:T(8,128)(2,1)} %fusion.8) | copy-start | bytes 393220
  185.0 9.0 %copy-start.28 = (bf16[64,1024]{1,0:T(8,128)(2,1)S(1)}, bf16[64,1024]{1,0:T(8,128)(2,1)}, u32[]{:S(2)}) copy-start(bf16[64,1024]{1,0:T(8,128)(2,1)} %fusion.9) | copy-start | bytes 393220
  187.1 8.0 %copy-start.27 = (bf16[64,1024]{1,0:T(8,128)(2,1)S(1)}, bf16[64,1024]{1,0:T(8,128)(2,1)}, u32[]{:S(2)}) copy-start(bf16[64,1024]{1,0:T(8,128)(2,1)} %fusion.10) | copy-start | bytes 393220
  189.2 7.0 %copy-start.26 = (bf16[64,1024]{1,0:T(8,128)(2,1)S(1)}, bf16[64,1024]{1,0:T(8,128)(2,1)}, u32[]{:S(2)}) copy-start(bf16[64,1024]{1,0:T(8,128)(2,1)} %fusion.11) | copy-start | bytes 393220
  190.4 7.0 %copy-start.25 = (bf16[64,1024]{1,0:T(8,128)(2,1)S(1)}, bf16[64,1024]{1,0:T(8,128)(2,1)}, u32[]{:S(2)}) copy-start(bf16[64,1024]{1,0:T(8,128)(2,1)} %fusion.12) | copy-start | bytes 393220
  210.5 4.6 %copy-start.24 = (bf16[64,1024]{1,0:T(8,128)(2,1)S(1)}, bf16[64,1024]{1,0:T(8,128)(2,1)}, u32[]{:S(2)}) copy-start(bf16[64,1024]{1,0:T(8,128)(2,1)} %fusion.29) | copy-start | bytes 393220
  216.3 2.6 %copy-start.33 = (bf16[1024,128]{1,0:T(8,128)(2,1)S(1)}, bf16[1024,128]{1,0:T(8,128)(2,1)}, u32[]{:S(2)}) copy-start(bf16[1024,128]{1,0:T(8,128)(2,1)} %param.6) | copy-start | bytes 786436
  217.4 2.8 %copy-start.22 = (bf16[2048,32]{1,0:T(8,128)(2,1)S(1)}, bf16[2048,32]{1,0:T(8,128)(2,1)}, u32[]{:S(2)}) copy-start(bf16[2048,32]{1,0:T(8,128)(2,1)} %reshape.171) | copy-start | bytes 393220
  218.8 1.7 copy-start.21
  220.2 1.0 copy-start.20
  220.5 1.1 copy-start.19
  221.3 1.1 copy-start.18
  221.6 1.1 copy-start.17
  222.3 1.1 copy-start.16
  222.7 1.1 copy-start.15
  223.4 1.1 copy-start.14
  223.8 1.1 copy-start.13
  224.5 1.1 copy-start.12
  224.8 1.1 copy-start.11
  225.6 1.1 copy-start.10
  225.9 1.1 copy-start.9
  226.7 1.1 copy-start.8
  227.0 1.1 copy-start.7
  227.8 1.1 copy-start.6
  228.1 1.1 copy-start.5
  228.8 1.1 copy-start.4
  229.2 1.1 copy-start.3
  229.9 1.1 copy-start.2
  230.2 1.1 copy-start.1
  231.0 1.1 copy-start
  233.4 1.0 copy-start.23
  233.4 1.0 copy-start.34
Sparse Core Ops, SparseCore 0:
  9.1 92.9 all-gather.4
  104.6 50.5 all-gather.2
where the time goes:
time: 243 us
  waiting for transfers between devices  142 us (58%)
  local copies, waits for them, and re-layouts  52.7 us (22%)
  matrix products  34.3 us (14%)
  between operations  13.8 us (6%)
    all_gather x1, waiting for transfers between devices, on_device(): right_whole = lax.all_gather(right_act, 'row', axis=0, tiled=True)  92.3 us
    all_gather x1, waiting for transfers between devices, on_device(): left_whole = lax.all_gather(left_act, 'col', axis=1, tiled=True)  48.6 us
    reshape x32, local copies, waits for them, and re-layouts, tile_rows(): outer_flat = outer_mean.reshape(row_count * col_count, channels)  36.6 us
    dot_general x32, matrix products, tile_rows(): lax.dot_general(left_major[channel], right_flat, (((0,), (0,)), ((), ()))...  22.7 us
    dot_general x32, matrix products, tile_rows(): jnp.dot(outer_flat, weight_three[channel], preferred_element_type=jnp.flo...  11.6 us
    unnamed x71, local copies, waits for them, and re-layouts  8.88 us
  transfers between devices with their start and end apart: 2, of which 2 were waited for; matrix products, arithmetic and copies ran while one was open for 2% of the time, Pallas kernels for 0%

commit v1 on v0

v1 whole, which is shorter than its diff:
```python
import jax
import jax.numpy as jnp
from jax import lax
from jax.experimental import pallas as pl
from jax.experimental.pallas import tpu as pltpu
from jax.sharding import PartitionSpec as P

C, CP, S = 32, 128, 512
MESH = pl.DeviceIdType.MESH
COMPUTE = True
COMM = True


def chunk_exchange(slabs, lane):
    a0, a1, a2, a3 = slabs
    low = lane < 64

    def swap64(a, b):
        return jnp.where(low, a, pltpu.roll(b, 64, 1)), jnp.where(low, pltpu.roll(a, 64, 1), b)

    def swap32(a, b):
        even = (lane % 64) < 32
        return jnp.where(even, a, pltpu.roll(b, 32, 1)), jnp.where(even, pltpu.roll(a, 96, 1), b)

    b0, b2 = swap64(a0, a2)
    b1, b3 = swap64(a1, a3)
    c0, c1 = swap32(b0, b1)
    c2, c3 = swap32(b2, b3)
    return c0, c1, c2, c3


def kernel(lt_hbm, rt_hbm, w_hbm, bias_ref, out_ref,
           lg, rp, rall, rt_v, w_v, wp, wide, pbuf,
           local_sems, ls, lr, rs, rr):
    row, col = lax.axis_index("row"), lax.axis_index("col")
    x, yl = row // 2, row % 2
    yh, z, c = col // 8, (col // 2) % 4, col % 2

    def dev(dx=0, dyl=0, dyh=0, dz=0, dc=0):
        xx, zz = (x + dx + 4) % 4, (z + dz + 4) % 4
        yyl = 1 - yl if dyl else yl
        yyh = 1 - yh if dyh else yh
        cc = 1 - c if dc else c
        return (xx * 2 + yyl, (yyh * 4 + zz) * 2 + cc)

    def lslot(dyh=0, dz=0, dc=0):
        q = dev(dyh=dyh, dz=dz, dc=dc)[1]
        return lg.at[pl.ds(pl.multiple_of(q * 128, 128), 128), :]

    def rslot(dx=0, dyl=0):
        r = dev(dx=dx, dyl=dyl)[0]
        return rp.at[pl.ds(pl.multiple_of(r * 512, 512), 512), :]

    load_l = pltpu.make_async_copy(lt_hbm, lslot(), local_sems.at[0])
    load_r = pltpu.make_async_copy(rt_hbm, rt_v, local_sems.at[1])
    load_w = pltpu.make_async_copy(w_hbm, w_v, local_sems.at[2])
    load_r.start()
    load_l.start()
    load_w.start()

    barrier = pltpu.get_barrier_semaphore()
    peers = [dev(dx=1), dev(dx=-1), dev(dyl=1), dev(dyh=1), dev(dz=1), dev(dz=-1), dev(dc=1)]
    for peer in peers:
        pl.semaphore_signal(barrier, inc=1, device_id=peer, device_id_type=MESH)

    lane_f = lax.broadcasted_iota(jnp.int32, (32, 128), 1)
    load_r.wait()
    wide[:, 0:64] = rt_v[...].astype(jnp.float32)
    own_r = rslot()
    for e in range(16):
        lo = wide[pl.ds(e, 32, stride=32), :]
        hi = wide[pl.ds(e + 16, 32, stride=32), :]
        both = jnp.where(lane_f < 64, lo, pltpu.roll(hi, 64, 1))
        own_r[pl.ds(e * 32, 32), :] = both.astype(jnp.bfloat16)
    load_l.wait()

    pl.semaphore_wait(barrier, len(peers))

    def lcopy(slot, to, k):
        return pltpu.make_async_remote_copy(
            src_ref=slot, dst_ref=slot, send_sem=ls.at[k], recv_sem=lr.at[k],
            device_id=to, device_id_type=MESH)

    def rcopy(slot, to, k):
        return pltpu.make_async_remote_copy(
            src_ref=slot, dst_ref=slot, send_sem=rs.at[k], recv_sem=rr.at[k],
            device_id=to, device_id_type=MESH)

    up, down, pair, sib = dev(dz=1), dev(dz=-1), dev(dyh=1), dev(dc=1)
    xup, xdown, ypair = dev(dx=1), dev(dx=-1), dev(dyl=1)
    if COMM:
        r_pair = rcopy(rslot(), ypair, 0)
        r_up, r_down = rcopy(rslot(), xup, 1), rcopy(rslot(), xdown, 2)
        l_pair = lcopy(lslot(), pair, 0)
        l_up, l_down = lcopy(lslot(), up, 1), lcopy(lslot(), down, 2)
        l_sib = lcopy(lslot(), sib, 7)
        for t in (r_pair, l_pair, r_up, r_down, l_up, l_down, l_sib):
            t.start()
        r_pair.wait_recv()
        r_pup, r_pdown = rcopy(rslot(dyl=1), xup, 3), rcopy(rslot(dyl=1), xdown, 4)
        r_pup.start()
        r_pdown.start()
        l_pair.wait_recv()
        l_pup, l_pdown = lcopy(lslot(dyh=1), up, 3), lcopy(lslot(dyh=1), down, 4)
        s_pair = lcopy(lslot(dyh=1), sib, 8)
        for t in (l_pup, l_pdown, s_pair):
            t.start()
        r_down.wait_recv()
        r_rel = rcopy(rslot(dx=1), xdown, 5)
        r_rel.start()
        l_down.wait_recv()
        l_rel = lcopy(lslot(dz=1), down, 5)
        s_a = lcopy(lslot(dz=1), sib, 9)
        l_rel.start()
        s_a.start()
        l_up.wait_recv()
        s_b = lcopy(lslot(dz=-1), sib, 10)
        s_b.start()
        r_up.wait_recv()
        r_pup.wait_recv()
        r_prel = rcopy(rslot(dx=-1, dyl=1), xup, 6)
        r_prel.start()
        l_pup.wait_recv()
        l_prel = lcopy(lslot(dyh=1, dz=-1), up, 6)
        s_c = lcopy(lslot(dyh=1, dz=-1), sib, 11)
        l_prel.start()
        s_c.start()
        l_pdown.wait_recv()
        s_d = lcopy(lslot(dyh=1, dz=1), sib, 12)
        s_d.start()
        l_rel.wait_recv()
        s_e = lcopy(lslot(dz=2), sib, 13)
        s_e.start()
        l_prel.wait_recv()
        s_f = lcopy(lslot(dyh=1, dz=2), sib, 14)
        s_f.start()
        for t in (r_pdown, r_rel, r_prel, l_sib, s_pair, s_a, s_b, s_c, s_d, s_e, s_f):
            t.wait_recv()
        for t in (r_pair, r_up, r_down, r_pup, r_pdown, r_rel, r_prel,
                  l_pair, l_up, l_down, l_sib, l_pup, l_pdown, l_rel, l_prel,
                  s_pair, s_a, s_b, s_c, s_d, s_e, s_f):
            t.wait_send()

    load_w.wait()
    if not COMPUTE:
        out_ref[...] = jnp.zeros_like(out_ref)
        return
    wide[...] = w_v[...].astype(jnp.float32)
    for e in range(32):
        wp[pl.ds(e * 32, 32), :] = wide[pl.ds(e, 32, stride=32), :].astype(jnp.bfloat16)

    lane = lax.broadcasted_iota(jnp.int32, (512, 128), 1)
    for xx in range(4):
        a = rp[xx * 1024:xx * 1024 + 512, :]
        b = rp[xx * 1024 + 512:xx * 1024 + 1024, :]
        rall[0:512, xx * 128:xx * 128 + 128] = jnp.where(lane < 64, a, pltpu.roll(b, 64, 1))
        rall[512:1024, xx * 128:xx * 128 + 128] = jnp.where(lane < 64, pltpu.roll(a, 64, 1), b)

    lane_s = lax.broadcasted_iota(jnp.int32, (32, 128), 1)

    def pair_step(p, carry):
        lblock = lg[pl.ds(pl.multiple_of(p * 256, 256), 256), :]
        for g in range(8):
            o = lax.dot_general(rall[g * 128:g * 128 + 128, :], lblock, (((1,), (1,)), ((), ())),
                                preferred_element_type=jnp.float32).astype(jnp.bfloat16)
            for h in range(2):
                slabs = [o[k * 32:k * 32 + 32, h * 128:h * 128 + 128] for k in range(4)]
                for i, t in enumerate(chunk_exchange(slabs, lane_s)):
                    pbuf[h * 128 + i * 32:h * 128 + i * 32 + 32, g * 128:g * 128 + 128] = t
        tile = jnp.dot(pbuf[...], wp[...], preferred_element_type=jnp.float32)
        out_ref[pl.ds(pl.multiple_of(p * 256, 256), 256), :] = tile * (1.0 / S) + bias_ref[...]
        return carry

    lax.fori_loop(0, 8, pair_step, 0)


def on_device(left_act, right_act, proj_weight, proj_bias):
    lt = jnp.transpose(left_act, (1, 2, 0)).reshape(128, S)
    rt = jnp.transpose(right_act, (1, 2, 0)).reshape(1024, 64)
    hbm, vmem = pl.BlockSpec(memory_space=pl.ANY), pl.BlockSpec(memory_space=pltpu.VMEM)
    out = pl.pallas_call(
        kernel,
        out_shape=jax.ShapeDtypeStruct((2048, CP), jnp.float32),
        in_specs=[hbm, hbm, hbm, vmem],
        out_specs=vmem,
        scratch_shapes=[
            pltpu.VMEM((2048, S), jnp.bfloat16),
            pltpu.VMEM((4096, 128), jnp.bfloat16),
            pltpu.VMEM((1024, S), jnp.bfloat16),
            pltpu.VMEM((1024, 64), jnp.bfloat16),
            pltpu.VMEM((1024, 128), jnp.bfloat16),
            pltpu.VMEM((1024, 128), jnp.bfloat16),
            pltpu.VMEM((1024, 128), jnp.float32),
            pltpu.VMEM((256, 1024), jnp.bfloat16),
            pltpu.SemaphoreType.DMA((3,)),
            pltpu.SemaphoreType.DMA((15,)),
            pltpu.SemaphoreType.DMA((15,)),
            pltpu.SemaphoreType.DMA((7,)),
            pltpu.SemaphoreType.DMA((7,)),
        ],
        compiler_params=pltpu.CompilerParams(
            collective_id=0, has_side_effects=True, vmem_limit_bytes=32 * 1024 * 1024
        ),
        cost_estimate=pl.CostEstimate(flops=2684354560, bytes_accessed=4 << 20, transcendentals=0),
    )(lt, rt, proj_weight, proj_bias.reshape(1, CP))
    return out.reshape(64, 32, CP)


def solution(mesh):
    return jax.shard_map(
        on_device,
        mesh=mesh,
        in_specs=(P(None, ("row", "col"), None), P("row", "col", None), P(), P()),
        out_specs=P("row", "col", None),
        check_vma=False,
    )
```

time: 243 us -> 40.9 us (0.17)
  waiting for transfers between devices: 142 us -> 0 us
  local copies, waits for them, and re-layouts: 52.7 us -> 4.43 us
  Pallas kernels: 0 us -> 36.2 us
  matrix products: 34.3 us -> 0 us
  between operations: 13.8 us -> 0.01 us
    all_gather x2 -> x0, waiting for transfers between devices: 141 us -> none  [the longest x1 92.3 us: on_device(): right_whole = lax.all_gather(right_act, 'row', axis=0, tiled=True)]
    reshape x32 -> x0, local copies, waits for them, and re-layouts: 36.6 us -> none  [tile_rows(): outer_flat = outer_mean.reshape(row_count * col_count, channels)]
    pallas_call x0 -> x1, Pallas kernels: none -> 36.2 us  [on_device(): pl.pallas_call(kernel, out_shape=jax.ShapeDtypeStruct((2048, CP), jnp.flo...]
    dot_general x64 -> x0, matrix products: 34.3 us -> none  [the longest x32 22.7 us: tile_rows(): lax.dot_general(left_major[channel], right_flat, (((0,), (0,)), ((), ()))...]
    all_gather x2 -> x0, local copies, waits for them, and re-layouts: 7.17 us -> none  [the longest x1 4.42 us: on_device(): right_whole = lax.all_gather(right_act, 'row', axis=0, tiled=True)]
    unnamed x71 -> x9, local copies, waits for them, and re-layouts: 8.88 us -> 4.43 us
  transfers between devices with their start and end apart: 2 -> 0, of which waited for: 2 -> 0; matrix products, arithmetic and copies ran while one was open for 2% -> 0% of each run, Pallas kernels for 0% -> 0%
where the time goes in v1:
time: 40.9 us; the launch traced here: 40.7 us
  Pallas kernels  36.2 us (89%)
  local copies, waits for them, and re-layouts  4.43 us (11%)
    pallas_call x1, Pallas kernels, on_device(): pl.pallas_call(kernel, out_shape=jax.ShapeDtypeStruct((2048, CP), jnp.flo...  36.2 us
    unnamed x9, local copies, waits for them, and re-layouts  4.43 us

profile of v1, /device:TPU:1, one launch (start us, length us, event | category | flops | bytes accessed | tf_op | source)
XLA Modules:
  0.0 40.7 jit_solution(17596614271513904610)
XLA Ops:
  0.0 0.0 copy-start.3
  0.0 0.7 %copy-done.3 = f32[128]{0:T(128)S(1)} copy-done((f32[128]{0:T(128)S(1)}, f32[128]{0:T(128)}, u32[]{:S(2)}) %copy-start.3) | copy-done | bytes 536
  0.7 0.0 copy-start
  0.7 0.9 %copy-done = bf16[64,32,32]{0,2,1:T(8,128)(2,1)S(1)} copy-done((bf16[64,32,32]{0,2,1:T(8,128)(2,1)S(1)}, bf16[64,32,32]{0,2,1:T(8,128)(2,1)}, u32[]{:S(2)}) %copy-start) | copy-done | bytes 131096
  1.6 0.0 copy-start.1
  1.6 0.9 %copy-done.1 = bf16[1024,128]{1,0:T(8,128)(2,1)S(1)} copy-done((bf16[1024,128]{1,0:T(8,128)(2,1)S(1)}, bf16[1024,128]{1,0:T(8,128)(2,1)}, u32[]{:S(2)}) %copy-start.1) | copy-done | bytes 262168
  2.6 0.0 copy-start.2
  2.6 0.9 %copy-done.2 = bf16[512,4,32]{0,2,1:T(8,128)(2,1)S(1)} copy-done((bf16[512,4,32]{0,2,1:T(8,128)(2,1)S(1)}, bf16[512,4,32]{0,2,1:T(8,128)(2,1)}, u32[]{:S(2)}) %copy-start.2) | copy-done | bytes 131096
  3.5 36.2 %shard_map.46 = f32[2048,128]{1,0:T(8,128)S(1)} custom-call(bf16[128,512]{1,0:T(8,128)(2,1)S(1)} %bitcast.10, bf16[1024,64]{1,0:T(8,128)(2,1)S(1)} %bitcast.9, bf16[1024,128]{1,0:T(8,128)(2,1)S(1)} %copy-done.1, f32[1,128]{1,0:T(1,128)S(1)} %bitcast.11), custom_call_target="tpu_custom_call" | custom-call | flops 2684354560 | bytes 4194304 | tf_op jit(solution)/shard_map/pallas_call | solution.py:181
  39.7 1.0 %copy.6 = f32[64,32,128]{2,1,0:T(8,128)} copy(f32[64,32,128]{2,1,0:T(8,128)S(1)} %bitcast.8) | data formatting | bytes 2097152
Async XLA Ops:
  0.0 0.7 %copy-start.3 = (f32[128]{0:T(128)S(1)}, f32[128]{0:T(128)}, u32[]{:S(2)}) copy-start(f32[128]{0:T(128)} %param.7) | copy-start | bytes 1540
  0.7 0.9 %copy-start = (bf16[64,32,32]{0,2,1:T(8,128)(2,1)S(1)}, bf16[64,32,32]{0,2,1:T(8,128)(2,1)}, u32[]{:S(2)}) copy-start(bf16[64,32,32]{0,2,1:T(8,128)(2,1)} %param.5) | copy-start | bytes 393220
  1.6 0.9 %copy-start.1 = (bf16[1024,128]{1,0:T(8,128)(2,1)S(1)}, bf16[1024,128]{1,0:T(8,128)(2,1)}, u32[]{:S(2)}) copy-start(bf16[1024,128]{1,0:T(8,128)(2,1)} %w_hbm.1) | copy-start | bytes 786436
  2.6 0.9 %copy-start.2 = (bf16[512,4,32]{0,2,1:T(8,128)(2,1)S(1)}, bf16[512,4,32]{0,2,1:T(8,128)(2,1)}, u32[]{:S(2)}) copy-start(bf16[512,4,32]{0,2,1:T(8,128)(2,1)} %param.4) | copy-start | bytes 393220

commit v2 on v0

v2 whole, which is shorter than its diff:
```python
import jax
import jax.numpy as jnp
from jax import lax
from jax.experimental import pallas as pl
from jax.experimental.pallas import tpu as pltpu
from jax.sharding import PartitionSpec as P

C, CP, S = 32, 128, 512
MESH = pl.DeviceIdType.MESH
NC = 2
NT = (((1,), (1,)), ((), ()))


def ranged(start, size):
    return pl.ds(pl.multiple_of(start, size), size)


def swap_halves(block):
    count = block.shape[0] // 64
    return jnp.concatenate([block[64 * (k ^ 1):64 * (k ^ 1) + 64] for k in range(count)], axis=0)


def product(a, b):
    return lax.dot_general(a, b, NT, preferred_element_type=jnp.float32)


def kernel(lt_hbm, rt_hbm, w_hbm, bias_hbm, out_ref,
           lg, rp, rall, lt_v, rt_v, w_v, bias_v, wp, wide, pb, wb, acc,
           local_sems, ls, lr, rs, rr, ss, sr):
    row, col = lax.axis_index("row"), lax.axis_index("col")
    x, yl = row // 2, row % 2
    yh, z, c = col // 8, (col // 2) % 4, col % 2

    def dev(dx=0, dyl=0, dyh=0, dz=0, dc=0):
        xx, zz = (x + dx + 4) % 4, (z + dz + 4) % 4
        yyl = 1 - yl if dyl else yl
        yyh = 1 - yh if dyh else yh
        cc = 1 - c if dc else c
        return (xx * 2 + yyl, (yyh * 4 + zz) * 2 + cc)

    def slot(kind, p=0, d=0, part=None):
        size = 128 if kind == "l" else 512
        index = dev(dyh=p, dz=d)[1] if kind == "l" else dev(dyl=p, dx=d)[0]
        buffer = lg if kind == "l" else rp
        if part is None:
            return buffer.at[ranged(index * size, size), :]
        piece = size // NC
        return buffer.at[ranged(index * size + part * piece, piece), :]

    load_l = pltpu.make_async_copy(lt_hbm, lt_v, local_sems.at[0])
    load_r = pltpu.make_async_copy(rt_hbm, rt_v, local_sems.at[1])
    load_w = pltpu.make_async_copy(w_hbm, w_v, local_sems.at[2])
    load_b = pltpu.make_async_copy(bias_hbm, bias_v, local_sems.at[3])
    for load in (load_l, load_r, load_w, load_b):
        load.start()

    barrier = pltpu.get_barrier_semaphore()
    peers = [dev(dx=1), dev(dx=-1), dev(dx=2), dev(dyl=1), dev(dyh=1),
             dev(dz=1), dev(dz=-1), dev(dz=2), dev(dc=1)]
    for peer in peers:
        pl.semaphore_signal(barrier, inc=1, device_id=peer, device_id_type=MESH)

    def interleave(a, b):
        low = lax.broadcasted_iota(jnp.int32, a.shape, 1) < 64
        return jnp.where(low, a, pltpu.roll(b, 64, 1)), jnp.where(low, pltpu.roll(a, 64, 1), b)

    load_l.wait()
    own_l = ranged(col * 128, 128)
    for t in range(2):
        even, odd = interleave(lt_v[:, t * 256:t * 256 + 128], lt_v[:, t * 256 + 128:t * 256 + 256])
        lg[own_l, t * 128:t * 128 + 128] = even
        lg[own_l, 256 + t * 128:256 + t * 128 + 128] = odd
    lane_f = lax.broadcasted_iota(jnp.int32, (32, 128), 1)

    def prepare_right():
        load_r.wait()
        wide[:, 0:64] = rt_v[...].astype(jnp.float32)
        for e in range(16):
            lo = wide[pl.ds(e, 32, stride=32), :]
            hi = wide[pl.ds(e + 16, 32, stride=32), :]
            both = jnp.where(lane_f < 64, lo, pltpu.roll(hi, 64, 1))
            rp[ranged(row * 512 + e * 32, 32), :] = both.astype(jnp.bfloat16)

    def prepare_weight():
        load_w.wait()
        load_b.wait()
        wide[...] = w_v[...].astype(jnp.float32)
        for e in range(32):
            wp[pl.ds(e * 32, 32), :] = wide[pl.ds(e, 32, stride=32), :].astype(jnp.bfloat16)
        zero = jnp.zeros((32, 128), jnp.bfloat16)
        for side in range(2):
            for e in range(16):
                for h in range(2):
                    source = (e + 16 * (h ^ side)) * 32
                    block = wp[source:source + 32, :]
                    for i2 in range(2):
                        r = side * 2048 + e * 128 + h * 64 + i2 * 32
                        wb[r:r + 32, i2 * 128:i2 * 128 + 128] = block
                        wb[r:r + 32, (1 - i2) * 128:(1 - i2) * 128 + 128] = zero

    def mover(send, recv):
        started = []

        def move(ref, to):
            k = len(started)
            copy = pltpu.make_async_remote_copy(
                src_ref=ref, dst_ref=ref, send_sem=send.at[k], recv_sem=recv.at[k],
                device_id=to, device_id_type=MESH)
            copy.start()
            started.append(copy)
            return copy
        return move, started

    lmove, lsent = mover(ls, lr)
    rmove, rsent = mover(rs, rr)
    smove, ssent = mover(ss, sr)
    move = {"l": lmove, "r": rmove}
    to = {"l": {"up": dev(dz=1), "down": dev(dz=-1), "far": dev(dz=2), "pair": dev(dyh=1)},
          "r": {"up": dev(dx=1), "down": dev(dx=-1), "far": dev(dx=2), "pair": dev(dyl=1)}}
    sib = dev(dc=1)
    parts = range(NC)
    ways = ("far", "up", "down")
    came = {"up": -1, "down": 1, "far": 2}
    g = {}
    sibs = {}

    def share(p, d):
        sibs[p, d] = smove(slot("l", p, d), sib)

    def send_pair(kind, k):
        g[kind, "pair", k] = move[kind](slot(kind, 0, 0, k), to[kind]["pair"])

    def send_own(kind, way):
        g[kind, way, 0] = move[kind](slot(kind), to[kind][way])

    def send_on(kind, k):
        g[kind, "pair", k].wait_recv()
        for way in ways:
            g[kind, way, 1, k] = move[kind](slot(kind, 1, 0, k), to[kind][way])

    prepare_right()
    pl.semaphore_wait(barrier, len(peers))
    for k in parts:
        send_pair("l", k)
        send_pair("r", k)
    for way in ("up", "down", "far"):
        send_own("l", way)
        send_own("r", way)
    share(0, 0)
    prepare_weight()

    def unpack(m):
        parity = yl if m == 0 else 1 - yl
        for t in range(2):
            a = rp[ranged((4 * t + parity) * 512, 512), :]
            b = rp[ranged((4 * t + 2 + parity) * 512, 512), :]
            low, high = interleave(a, b)
            rall[0:512, m * 256 + t * 128:m * 256 + t * 128 + 128] = low
            rall[512:1024, m * 256 + t * 128:m * 256 + t * 128 + 128] = high

    lanes = [ranged(yl * 256, 256), ranged((1 - yl) * 256, 256)]
    lowlane = lax.broadcasted_iota(jnp.int32, (512, 256), 1) % 128 < 64

    def mix(o_lo, o_hi, rows):
        o_lo, o_hi = o_lo.astype(jnp.bfloat16), o_hi.astype(jnp.bfloat16)
        for side, mixed in enumerate((jnp.where(lowlane, o_lo, o_hi), jnp.where(lowlane, o_hi, o_lo))):
            for e in range(16):
                for t, r in enumerate(rows):
                    pb[side, r:r + 32, e * 128:e * 128 + 128] = mixed[e * 32:e * 32 + 32, t * 128:t * 128 + 128]

    def project(first, blocks):
        count = 32 * len(blocks)
        for side in range(2):
            res = jnp.dot(pb[side, first:first + count, :], wb[side * 2048:side * 2048 + 2048, :],
                          preferred_element_type=jnp.float32)
            for t, b in enumerate(blocks):
                for i2 in range(2):
                    out_ref[ranged(b * 128 + (2 * side + i2) * 32, 32), :] = (
                        res[t * 32:t * 32 + 32, i2 * 128:i2 * 128 + 128] * (1.0 / S) + bias_v[...])

    for k in parts:
        send_on("l", k)
        send_on("r", k)
    share(1, 0)
    for way in ways:
        g["l", way, 0].wait_recv()
        share(0, came[way])
        g["r", way, 0].wait_recv()
    for p, d in ((0, 0), (0, 2), (0, -1), (0, 1)):
        sibs[p, d].wait_recv()
    unpack(0)
    for t in range(4):
        block = lg[ranged(yh * 1024 + t * 256, 256), lanes[0]]
        acc[2 * t] = product(rall[0:512, 0:256], block)
        acc[2 * t + 1] = product(rall[512:1024, 0:256], swap_halves(block))

    for way in ways:
        for k in parts:
            g["l", way, 1, k].wait_recv()
        share(1, came[way])
        for k in parts:
            g["r", way, 1, k].wait_recv()
    unpack(1)
    for t in range(4):
        block = lg[ranged(yh * 1024 + t * 256, 256), lanes[1]]
        mix(acc[2 * t] + product(rall[0:512, 256:512], block),
            acc[2 * t + 1] + product(rall[512:1024, 256:512], swap_halves(block)),
            (t * 64, t * 64 + 32))
    project(0, [yh * 8 + t for t in range(8)])

    other = (1 - yh) * 8
    for who in range(2):
        core = c if who == 0 else 1 - c
        if who == 1:
            for d in (0, 2, -1, 1):
                sibs[1, d].wait_recv()
        for t in range(2):
            block = jnp.concatenate(
                [jnp.concatenate([lg[ranged((other + (2 * t + u) * 2 + core) * 128, 128), lanes[m]] for m in range(2)], axis=1)
                 for u in range(2)], axis=0)
            r = 256 + who * 128 + t * 64
            mix(product(rall[0:512, :], block), product(rall[512:1024, :], swap_halves(block)), (r, r + 32))
    project(256, [other + t * 2 + (c if who == 0 else 1 - c) for who in range(2) for t in range(4)])
    for copy in lsent + rsent + ssent:
        copy.wait_send()


def on_device(left_act, right_act, proj_weight, proj_bias):
    lt = jnp.transpose(left_act, (1, 2, 0)).reshape(128, S)
    rt = jnp.transpose(right_act, (1, 2, 0)).reshape(1024, 64)
    bias = proj_bias.reshape(1, CP)
    hbm, vmem = pl.BlockSpec(memory_space=pltpu.HBM), pl.BlockSpec(memory_space=pltpu.VMEM)
    dma = pltpu.SemaphoreType.DMA
    arrays = [pltpu.with_memory_space_constraint(a, pltpu.HBM) for a in (lt, rt, proj_weight, bias)]
    out = pl.pallas_call(
        kernel,
        out_shape=jax.ShapeDtypeStruct((2048, CP), jnp.float32),
        in_specs=[hbm, hbm, hbm, hbm],
        out_specs=vmem,
        scratch_shapes=[
            pltpu.VMEM((2048, S), jnp.bfloat16),
            pltpu.VMEM((4096, 128), jnp.bfloat16),
            pltpu.VMEM((1024, S), jnp.bfloat16),
            pltpu.VMEM((128, S), jnp.bfloat16),
            pltpu.VMEM((1024, 64), jnp.bfloat16),
            pltpu.VMEM((1024, 128), jnp.bfloat16),
            pltpu.VMEM((1, 128), jnp.float32),
            pltpu.VMEM((1024, 128), jnp.bfloat16),
            pltpu.VMEM((1024, 128), jnp.float32),
            pltpu.VMEM((2, 512, 2048), jnp.bfloat16),
            pltpu.VMEM((4096, 256), jnp.bfloat16),
            pltpu.VMEM((8, 512, 256), jnp.float32),
            dma((4,)), dma((16,)), dma((16,)), dma((16,)), dma((16,)), dma((8,)), dma((8,)),
        ],
        compiler_params=pltpu.CompilerParams(
            collective_id=0, has_side_effects=True, vmem_limit_bytes=40 * 1024 * 1024
        ),
        cost_estimate=pl.CostEstimate(flops=3221225472, bytes_accessed=4 << 20, transcendentals=0),
    )(*arrays)
    return out.reshape(64, 32, CP)


def solution(mesh):
    return jax.shard_map(
        on_device,
        mesh=mesh,
        in_specs=(P(None, ("row", "col"), None), P("row", "col", None), P(), P()),
        out_specs=P("row", "col", None),
        check_vma=False,
    )
```

time: 243 us -> 24.7 us (0.10)
  waiting for transfers between devices: 142 us -> 0 us
  local copies, waits for them, and re-layouts: 52.7 us -> 0.97 us
  matrix products: 34.3 us -> 0 us
  Pallas kernels: 0 us -> 23.6 us
  between operations: 13.8 us -> 0.01 us
    all_gather x2 -> x0, waiting for transfers between devices: 141 us -> none  [the longest x1 92.3 us: on_device(): right_whole = lax.all_gather(right_act, 'row', axis=0, tiled=True)]
    reshape x32 -> x0, local copies, waits for them, and re-layouts: 36.6 us -> none  [tile_rows(): outer_flat = outer_mean.reshape(row_count * col_count, channels)]
    dot_general x64 -> x0, matrix products: 34.3 us -> none  [the longest x32 22.7 us: tile_rows(): lax.dot_general(left_major[channel], right_flat, (((0,), (0,)), ((), ()))...]
    pallas_call x0 -> x1, Pallas kernels: none -> 23.6 us  [on_device(): pl.pallas_call(kernel, out_shape=jax.ShapeDtypeStruct((2048, CP), jnp.flo...]
    unnamed x71 -> x1, local copies, waits for them, and re-layouts: 8.88 us -> 0.97 us
    all_gather x2 -> x0, local copies, waits for them, and re-layouts: 7.17 us -> none  [the longest x1 4.42 us: on_device(): right_whole = lax.all_gather(right_act, 'row', axis=0, tiled=True)]
  transfers between devices with their start and end apart: 2 -> 0, of which waited for: 2 -> 0; matrix products, arithmetic and copies ran while one was open for 2% -> 0% of each run, Pallas kernels for 0% -> 0%
where the time goes in v2:
time: 24.7 us; the launch traced here: 24.5 us
  Pallas kernels  23.6 us (96%)
  local copies, waits for them, and re-layouts  0.97 us (4%)
    pallas_call x1, Pallas kernels, on_device(): pl.pallas_call(kernel, out_shape=jax.ShapeDtypeStruct((2048, CP), jnp.flo...  23.6 us
    unnamed x1, local copies, waits for them, and re-layouts  0.97 us

profile of v2, /device:TPU:1, one launch (start us, length us, event | category | flops | bytes accessed | tf_op | source)
XLA Modules:
  0.0 24.5 jit_solution(6822142368511834849)
XLA Ops:
  0.0 23.6 %shard_map.46 = f32[2048,128]{1,0:T(8,128)S(1)} custom-call(bf16[128,512]{1,0:T(8,128)(2,1)} %bitcast.10, bf16[1024,64]{1,0:T(8,128)(2,1)} %bitcast.9, bf16[1024,128]{1,0:T(8,128)(2,1)} %w_hbm.1, f32[1,128]{1,0:T(1,128)} %bitcast.11), custom_call_target="tpu_custom_call" | custom-call | flops 3221225472 | bytes 4194304 | tf_op jit(solution)/shard_map/pallas_call | solution.py:235
  23.6 1.0 %copy.6 = f32[64,32,128]{2,1,0:T(8,128)} copy(f32[64,32,128]{2,1,0:T(8,128)S(1)} %bitcast.8) | data formatting | bytes 2097152

commit v3 on v2

--- a/solution.py
+++ b/solution.py
@@ -7,7 +7,8 @@
 
 C, CP, S = 32, 128, 512
 MESH = pl.DeviceIdType.MESH
-NC = 2
+PARTS = {"l": ((0, 3), (3, 5)), "r": ((0, 3), (3, 5))}
+AROUND = {"l": (1,), "r": (1,)}
 NT = (((1,), (1,)), ((), ()))
 
 
@@ -44,8 +45,9 @@
         buffer = lg if kind == "l" else rp
         if part is None:
             return buffer.at[ranged(index * size, size), :]
-        piece = size // NC
-        return buffer.at[ranged(index * size + part * piece, piece), :]
+        first, count = PARTS[kind][part]
+        step = size // 8
+        return buffer.at[pl.ds(pl.multiple_of(index * size + first * step, step), count * step), :]
 
     load_l = pltpu.make_async_copy(lt_hbm, lt_v, local_sems.at[0])
     load_r = pltpu.make_async_copy(rt_hbm, rt_v, local_sems.at[1])
@@ -118,32 +120,42 @@
     to = {"l": {"up": dev(dz=1), "down": dev(dz=-1), "far": dev(dz=2), "pair": dev(dyh=1)},
           "r": {"up": dev(dx=1), "down": dev(dx=-1), "far": dev(dx=2), "pair": dev(dyl=1)}}
     sib = dev(dc=1)
-    parts = range(NC)
+    parts = {kind: range(len(PARTS[kind])) for kind in PARTS}
+    most = range(max(len(parts["l"]), len(parts["r"])))
     ways = ("far", "up", "down")
     came = {"up": -1, "down": 1, "far": 2}
     g = {}
     sibs = {}
 
-    def share(p, d):
-        sibs[p, d] = smove(slot("l", p, d), sib)
+    def share(p, d, k=None):
+        sibs[p, d, k] = smove(slot("l", p, d, k), sib)
 
     def send_pair(kind, k):
         g[kind, "pair", k] = move[kind](slot(kind, 0, 0, k), to[kind]["pair"])
 
-    def send_own(kind, way):
-        g[kind, way, 0] = move[kind](slot(kind), to[kind][way])
+    def send_own(kind, way, k=None):
+        key = (kind, way, 0) if k is None else (kind, way, 0, k)
+        g[key] = move[kind](slot(kind, 0, 0, k), to[kind][way])
 
     def send_on(kind, k):
         g[kind, "pair", k].wait_recv()
         for way in ways:
-            g[kind, way, 1, k] = move[kind](slot(kind, 1, 0, k), to[kind][way])
+            if way != "far" or k not in AROUND[kind]:
+                g[kind, way, 1, k] = move[kind](slot(kind, 1, 0, k), to[kind][way])
+
+    def send_around(kind, k):
+        g[kind, "far", 0, k].wait_recv()
+        g[kind, "far", 1, k] = move[kind](slot(kind, 0, 2, k), to[kind]["pair"])
 
     prepare_right()
     pl.semaphore_wait(barrier, len(peers))
-    for k in parts:
-        send_pair("l", k)
-        send_pair("r", k)
-    for way in ("up", "down", "far"):
+    for kind in ("l", "r"):
+        for k in parts[kind]:
+            send_pair(kind, k)
+    for kind in ("l", "r"):
+        for k in sorted(parts[kind], key=lambda k: k not in AROUND[kind]):
+            send_own(kind, "far", k)
+    for way in ("up", "down"):
         send_own("l", way)
         send_own("r", way)
     share(0, 0)
@@ -178,42 +190,63 @@
                     out_ref[ranged(b * 128 + (2 * side + i2) * 32, 32), :] = (
                         res[t * 32:t * 32 + 32, i2 * 128:i2 * 128 + 128] * (1.0 / S) + bias_v[...])
 
-    for k in parts:
-        send_on("l", k)
-        send_on("r", k)
+    for k in most:
+        for kind in ("l", "r"):
+            if k in parts[kind]:
+                send_on(kind, k)
+    for kind in ("l", "r"):
+        for k in AROUND[kind]:
+            send_around(kind, k)
     share(1, 0)
     for way in ways:
-        g["l", way, 0].wait_recv()
-        share(0, came[way])
-        g["r", way, 0].wait_recv()
-    for p, d in ((0, 0), (0, 2), (0, -1), (0, 1)):
-        sibs[p, d].wait_recv()
+        for kind in ("l", "r"):
+            if way == "far":
+                for k in parts[kind]:
+                    if k not in AROUND[kind]:
+                        g[kind, way, 0, k].wait_recv()
+            else:
+                g[kind, way, 0].wait_recv()
+            if kind == "l":
+                share(0, came[way])
+    for d in (0, 2, -1, 1):
+        sibs[0, d, None].wait_recv()
     unpack(0)
     for t in range(4):
         block = lg[ranged(yh * 1024 + t * 256, 256), lanes[0]]
         acc[2 * t] = product(rall[0:512, 0:256], block)
         acc[2 * t + 1] = product(rall[512:1024, 0:256], swap_halves(block))
 
-    for way in ways:
-        for k in parts:
+    def pass_on(k):
+        for way in ways:
             g["l", way, 1, k].wait_recv()
-        share(1, came[way])
-        for k in parts:
-            g["r", way, 1, k].wait_recv()
-    unpack(1)
-    for t in range(4):
+            share(1, came[way], k)
+
+    def finish(t):
         block = lg[ranged(yh * 1024 + t * 256, 256), lanes[1]]
         mix(acc[2 * t] + product(rall[0:512, 256:512], block),
             acc[2 * t + 1] + product(rall[512:1024, 256:512], swap_halves(block)),
             (t * 64, t * 64 + 32))
+
+    for k in parts["l"]:
+        pass_on(k)
+    for k in parts["r"]:
+        for way in ways:
+            g["r", way, 1, k].wait_recv()
+    unpack(1)
+    for t in range(0):
+        finish(t)
+    for t in range(0, 4):
+        finish(t)
     project(0, [yh * 8 + t for t in range(8)])
 
     other = (1 - yh) * 8
     for who in range(2):
         core = c if who == 0 else 1 - c
         if who == 1:
-            for d in (0, 2, -1, 1):
-                sibs[1, d].wait_recv()
+            sibs[1, 0, None].wait_recv()
+            for k in parts["l"]:
+                for d in (2, -1, 1):
+                    sibs[1, d, k].wait_recv()
         for t in range(2):
             block = jnp.concatenate(
                 [jnp.concatenate([lg[ranged((other + (2 * t + u) * 2 + core) * 128, 128), lanes[m]] for m in range(2)], axis=1)
@@ -250,7 +283,7 @@
             pltpu.VMEM((2, 512, 2048), jnp.bfloat16),
             pltpu.VMEM((4096, 256), jnp.bfloat16),
             pltpu.VMEM((8, 512, 256), jnp.float32),
-            dma((4,)), dma((16,)), dma((16,)), dma((16,)), dma((16,)), dma((8,)), dma((8,)),
+            dma((4,)), dma((20,)), dma((20,)), dma((20,)), dma((20,)), dma((20,)), dma((20,)),
         ],
         compiler_params=pltpu.CompilerParams(
             collective_id=0, has_side_effects=True, vmem_limit_bytes=40 * 1024 * 1024

time: 24.7 us -> 23.1 us (0.935)
  Pallas kernels: 23.6 us -> 22 us
    pallas_call x1, Pallas kernels: 23.6 us -> 22 us  [on_device(): pl.pallas_call(kernel, out_shape=jax.ShapeDtypeStruct((2048, CP), jnp.flo...]
where the time goes in v3:
time: 23.1 us; the launch traced here: 23 us
  Pallas kernels  22 us (95%)
  local copies, waits for them, and re-layouts  0.97 us (4%)
    pallas_call x1, Pallas kernels, on_device(): pl.pallas_call(kernel, out_shape=jax.ShapeDtypeStruct((2048, CP), jnp.flo...  22 us
    unnamed x1, local copies, waits for them, and re-layouts  0.97 us

profile of v3, /device:TPU:1, one launch (start us, length us, event | category | flops | bytes accessed | tf_op | source)
XLA Modules:
  0.0 23.0 jit_solution(10318630304508316634)
XLA Ops:
  0.0 22.0 %shard_map.46 = f32[2048,128]{1,0:T(8,128)S(1)} custom-call(bf16[128,512]{1,0:T(8,128)(2,1)} %bitcast.10, bf16[1024,64]{1,0:T(8,128)(2,1)} %bitcast.9, bf16[1024,128]{1,0:T(8,128)(2,1)} %w_hbm.1, f32[1,128]{1,0:T(1,128)} %bitcast.11), custom_call_target="tpu_custom_call" | custom-call | flops 3221225472 | bytes 4194304 | tf_op jit(solution)/shard_map/pallas_call | solution.py:268
  22.0 1.0 %copy.6 = f32[64,32,128]{2,1,0:T(8,128)} copy(f32[64,32,128]{2,1,0:T(8,128)S(1)} %bitcast.8) | data formatting | bytes 2097152

commit v4 on v3

--- a/solution.py
+++ b/solution.py
@@ -253,7 +253,7 @@
                  for u in range(2)], axis=0)
             r = 256 + who * 128 + t * 64
             mix(product(rall[0:512, :], block), product(rall[512:1024, :], swap_halves(block)), (r, r + 32))
-    project(256, [other + t * 2 + (c if who == 0 else 1 - c) for who in range(2) for t in range(4)])
+        project(256 + who * 128, [other + t * 2 + core for t in range(4)])
     for copy in lsent + rsent + ssent:
         copy.wait_send()
 

time: 23.1 us -> 22.9 us (level)
  no operation moved by 1% of the time
where the time goes in v4:
time: 22.9 us; the launch traced here: 22.8 us
  Pallas kernels  21.8 us (95%)
  local copies, waits for them, and re-layouts  0.97 us (4%)
    pallas_call x1, Pallas kernels, on_device(): pl.pallas_call(kernel, out_shape=jax.ShapeDtypeStruct((2048, CP), jnp.flo...  21.8 us
    unnamed x1, local copies, waits for them, and re-layouts  0.97 us

profile of v4, /device:TPU:1, one launch (start us, length us, event | category | flops | bytes accessed | tf_op | source)
XLA Modules:
  0.0 22.8 jit_solution(78835027186253443)
XLA Ops:
  0.0 21.8 %shard_map.46 = f32[2048,128]{1,0:T(8,128)S(1)} custom-call(bf16[128,512]{1,0:T(8,128)(2,1)} %bitcast.10, bf16[1024,64]{1,0:T(8,128)(2,1)} %bitcast.9, bf16[1024,128]{1,0:T(8,128)(2,1)} %w_hbm.1, f32[1,128]{1,0:T(1,128)} %bitcast.11), custom_call_target="tpu_custom_call" | custom-call | flops 3221225472 | bytes 4194304 | tf_op jit(solution)/shard_map/pallas_call | solution.py:268
  21.8 1.0 %copy.6 = f32[64,32,128]{2,1,0:T(8,128)} copy(f32[64,32,128]{2,1,0:T(8,128)S(1)} %bitcast.8) | data formatting | bytes 2097152

commit v5 on v4

--- a/solution.py
+++ b/solution.py
@@ -216,10 +216,9 @@
         acc[2 * t] = product(rall[0:512, 0:256], block)
         acc[2 * t + 1] = product(rall[512:1024, 0:256], swap_halves(block))
 
-    def pass_on(k):
-        for way in ways:
-            g["l", way, 1, k].wait_recv()
-            share(1, came[way], k)
+    def pass_on(way, k):
+        g["l", way, 1, k].wait_recv()
+        share(1, came[way], k)
 
     def finish(t):
         block = lg[ranged(yh * 1024 + t * 256, 256), lanes[1]]
@@ -227,8 +226,8 @@
             acc[2 * t + 1] + product(rall[512:1024, 256:512], swap_halves(block)),
             (t * 64, t * 64 + 32))
 
-    for k in parts["l"]:
-        pass_on(k)
+    for way, k in (("far", 0), ("far", 1), ("up", 0), ("down", 0), ("up", 1), ("down", 1)):
+        pass_on(way, k)
     for k in parts["r"]:
         for way in ways:
             g["r", way, 1, k].wait_recv()

time: 22.9 us -> 23 us (level)
  no operation moved by 1% of the time
where the time goes in v5:
time: 23 us; the launch traced here: 22.8 us
  Pallas kernels  21.9 us (95%)
  local copies, waits for them, and re-layouts  0.97 us (4%)
    pallas_call x1, Pallas kernels, on_device(): pl.pallas_call(kernel, out_shape=jax.ShapeDtypeStruct((2048, CP), jnp.flo...  21.9 us
    unnamed x1, local copies, waits for them, and re-layouts  0.97 us

profile of v5, /device:TPU:1, one launch (start us, length us, event | category | flops | bytes accessed | tf_op | source)
XLA Modules:
  0.0 22.8 jit_solution(11792809713258476513)
XLA Ops:
  0.0 21.9 %shard_map.46 = f32[2048,128]{1,0:T(8,128)S(1)} custom-call(bf16[128,512]{1,0:T(8,128)(2,1)} %bitcast.10, bf16[1024,64]{1,0:T(8,128)(2,1)} %bitcast.9, bf16[1024,128]{1,0:T(8,128)(2,1)} %w_hbm.1, f32[1,128]{1,0:T(1,128)} %bitcast.11), custom_call_target="tpu_custom_call" | custom-call | flops 3221225472 | bytes 4194304 | tf_op jit(solution)/shard_map/pallas_call | solution.py:267
  21.9 1.0 %copy.6 = f32[64,32,128]{2,1,0:T(8,128)} copy(f32[64,32,128]{2,1,0:T(8,128)S(1)} %bitcast.8) | data formatting | bytes 2097152

commit v6 on v4

--- a/solution.py
+++ b/solution.py
@@ -227,6 +227,10 @@
             acc[2 * t + 1] + product(rall[512:1024, 256:512], swap_halves(block)),
             (t * 64, t * 64 + 32))
 
+    early = [g[key] for key in g if key[1] == "pair" or key[2] == 0] + [sibs[key] for key in sibs if key[0] == 0]
+    left = {id(copy) for copy in early}
+    for copy in early:
+        copy.wait_send()
     for k in parts["l"]:
         pass_on(k)
     for k in parts["r"]:
@@ -255,7 +259,8 @@
             mix(product(rall[0:512, :], block), product(rall[512:1024, :], swap_halves(block)), (r, r + 32))
         project(256 + who * 128, [other + t * 2 + core for t in range(4)])
     for copy in lsent + rsent + ssent:
-        copy.wait_send()
+        if id(copy) not in left:
+            copy.wait_send()
 
 
 def on_device(left_act, right_act, proj_weight, proj_bias):

time: 22.9 us -> 22.9 us (level)
  no operation moved by 1% of the time
where the time goes in v6:
time: 22.9 us; the launch traced here: 22.7 us
  Pallas kernels  21.8 us (95%)
  local copies, waits for them, and re-layouts  0.97 us (4%)
    pallas_call x1, Pallas kernels, on_device(): pl.pallas_call(kernel, out_shape=jax.ShapeDtypeStruct((2048, CP), jnp.flo...  21.8 us
    unnamed x1, local copies, waits for them, and re-layouts  0.97 us

profile of v6, /device:TPU:1, one launch (start us, length us, event | category | flops | bytes accessed | tf_op | source)
XLA Modules:
  0.0 22.7 jit_solution(11565415073378818451)
XLA Ops:
  0.0 21.8 %shard_map.46 = f32[2048,128]{1,0:T(8,128)S(1)} custom-call(bf16[128,512]{1,0:T(8,128)(2,1)} %bitcast.10, bf16[1024,64]{1,0:T(8,128)(2,1)} %bitcast.9, bf16[1024,128]{1,0:T(8,128)(2,1)} %w_hbm.1, f32[1,128]{1,0:T(1,128)} %bitcast.11), custom_call_target="tpu_custom_call" | custom-call | flops 3221225472 | bytes 4194304 | tf_op jit(solution)/shard_map/pallas_call | solution.py:273
  21.8 1.0 %copy.6 = f32[64,32,128]{2,1,0:T(8,128)} copy(f32[64,32,128]{2,1,0:T(8,128)S(1)} %bitcast.8) | data formatting | bytes 2097152
